TPU v7x, 32 devices: a whole 2x2x4 slice. The times are simulated.
32 devices in a mesh: site: 4 (over z), dev: 8 (over y, x, core).
Axes of the slice: x: 2, y: 2, z: 4, core: 2. Of those that a mesh axis runs over, the one named last changes fastest.
Arguments:
- tokens: bfloat16 [4, 1024, 8192], P('site', 'dev'), may hold values from -6 to 6
- cotangent: bfloat16 [4, 1024, 64], P('site', 'dev'), may hold values from -0.119628906 to 0.119628906
- weight: bfloat16 [64, 8192], P('dev'), may hold values from -0.0625 to 0.0625
- momentum: float32 [4, 64, 8192], P('site', 'dev'), may hold values from -6 to 6
- kept_index: int32 [4, 64, 128, 16], P(None, 'dev'), may hold values from 0 to 63, all different within a row
Outputs:
- scores: bfloat16 [4, 1024, 64], P('site', 'dev')
- momentum_out: float32 [4, 64, 8192], P('site', 'dev')
Inputs may be any that keep to these rules, and one draw needn't show every extreme that they name: `kept_index`: the 16 indices of one block and site are all different.
All inputs are finite; a program needn't handle non-finite values.
Results may differ from a plain program's by a relative error of at most 0.022.
Values may be sent and summed in bfloat16 or wider, within the bound.
A program may use at most 64 MiB of HBM per device.

v0:
```python
import jax
import jax.numpy as jnp
from jax import lax
from jax.sharding import PartitionSpec as P

momentum_decay = 0.999
step_size = 0.01


def pair_table():
    lanes = jnp.arange(128)
    freq = (lanes % 64)[:, None].astype(jnp.float32)
    place = (lanes % 64)[None, :].astype(jnp.float32)
    factor = jnp.where(freq == 0.0, jnp.sqrt(1.0 / 64.0), jnp.sqrt(2.0 / 64.0)).astype(jnp.float32)
    same_half = ((lanes // 64)[:, None] == (lanes // 64)[None, :]).astype(jnp.float32)
    return factor * jnp.cos(jnp.pi * (2.0 * place + 1.0) * freq / 128.0) * same_half


def spread_index(block_index):
    row_count, block_count, kept = block_index.shape
    paired = block_index.reshape(row_count, block_count // 2, 2, kept)
    offsets = (jnp.arange(2) * 64)[None, None, :, None]
    return (paired + offsets).reshape(row_count, block_count // 2, 2 * kept)


def shards(tokens, cotangent, weight, momentum, kept_index):
    local_tokens = tokens[0]
    local_cotan = cotangent[0]
    row_total = weight.shape[0]
    grad = lax.psum_scatter(
        lax.dot_general(
            local_cotan, local_tokens, (((0,), (0,)), ((), ())), preferred_element_type=jnp.float32
        ).astype(jnp.bfloat16),
        "dev",
        scatter_dimension=0,
        tiled=True,
    ).astype(jnp.float32)
    width = grad.shape[1]
    table = pair_table()
    lane_iota = jnp.arange(128)
    raised = momentum_decay * momentum[0] + grad
    coefs = jnp.dot(raised.reshape(-1, 128), table.T, precision=lax.Precision.HIGHEST)
    coefs = coefs.reshape(row_total, width // 128, 128)
    site_number = lax.axis_index("site")
    own_index = lax.dynamic_index_in_dim(kept_index, site_number, 0, keepdims=False)
    own_lanes = spread_index(own_index)
    keep_mask = jnp.any(own_lanes[..., None] == lane_iota, axis=2).astype(jnp.float32)
    picked = coefs * keep_mask
    reverted = jnp.dot(picked.reshape(-1, 128), table, precision=lax.Precision.HIGHEST)
    momentum_new = raised - reverted.reshape(row_total, width)
    matches = own_lanes[..., None] == lane_iota
    kept_values = jnp.sum(jnp.where(matches, coefs[:, :, None, :], 0.0), axis=3).astype(
        jnp.bfloat16
    )
    gathered = lax.all_gather(kept_values.reshape(1, row_total, -1), "site", axis=0, tiled=True)
    site_total = gathered.shape[0]

    def add_site(site_step, running):
        lanes_here = spread_index(kept_index[site_step])
        values_here = gathered[site_step].reshape(lanes_here.shape).astype(jnp.float32)
        placed = jnp.where(lanes_here[..., None] == lane_iota, values_here[..., None], 0.0)
        return running + jnp.sum(placed, axis=2)

    total = lax.fori_loop(0, site_total, add_site, jnp.zeros(coefs.shape, jnp.float32))
    decoded = jnp.dot(total.reshape(-1, 128), table, precision=lax.Precision.HIGHEST)
    decoded = decoded.reshape(row_total, width)
    new_weight = (weight.astype(jnp.float32) - step_size * decoded).astype(jnp.bfloat16)
    scores = lax.dot_general(
        local_tokens,
        lax.all_gather(new_weight, "dev", axis=0, tiled=True),
        (((1,), (1,)), ((), ())),
        preferred_element_type=jnp.float32,
    ).astype(jnp.bfloat16)
    return (scores[None], momentum_new[None])


def solution(mesh):
    placed = (
        P("site", "dev", None),
        P("site", "dev", None),
        P("dev", None),
        P("site", "dev", None),
        P(None, "dev", None, None),
    )
    return jax.shard_map(
        shards,
        mesh=mesh,
        in_specs=placed,
        out_specs=(P("site", "dev", None), P("site", "dev", None)),
        check_vma=False,
    )
```

profile of v0, /device:TPU:1, one launch (start us, length us, event | category | flops | bytes accessed | tf_op | source)
XLA Modules:
  0.0 136.0 jit_solution(11054411128796291615)
XLA Ops:
  7.2 1.5 %copy-done = bf16[1,128,8192]{2,1,0:T(8,128)(2,1)S(1)} copy-done((bf16[1,128,8192]{2,1,0:T(8,128)(2,1)S(1)}, bf16[1,128,8192]{2,1,0:T(8,128)(2,1)}, u32[]{:S(2)}) %copy-start) | copy-done | bytes 2097176
  8.8 2.1 %convolution_convert_fusion = bf16[64,8192]{1,0:T(8,128)(2,1)} fusion(bf16[1,128,8192]{2,1,0:T(8,128)(2,1)S(1)} %copy-done, bf16[1,128,64]{1,2,0:T(8,128)(2,1)} %param.8), kind=kOutput, calls=%fused_computation.8 | convolution fusion | flops 134742016 | bytes 3162112 | tf_op jit(solution)/shard_map/dot_general | solution.py:31
  11.0 0.8 constant_dynamic-slice_fusion.1
  11.8 0.2 copy.11
  12.4 3.6 %fusion.2 = pred[8,64,128]{2,1,0:T(8,128)(4,1)} fusion(s32[8,64,32]{2,1,0:T(8,128)S(1)} %broadcast_add_fusion.1), kind=kLoop, calls=%fused_computation.11 | loop fusion | flops 4128768 | bytes 131072 | tf_op jit(solution)/shard_map/reduce_or | solution.py:47
  16.0 33.2 %reduce-scatter.2.cloned.1.call-done = bf16[8,8192]{1,0:T(8,128)(2,1)} async-done(((bf16[64,8192]{1,0:T(8,128)(2,1)}), bf16[8,8192]{1,0:T(8,128)(2,1)}) %reduce-scatter.2.cloned.1.call-update) | async-done | bytes 131088 | tf_op jit(solution)/shard_map/reduce_scatter | solution.py:30
  49.2 0.9 bitcast_add_fusion
  50.2 0.7 fusion.15
  50.9 0.7 copy-done.1
  51.6 5.1 %select_reduce_fusion.1 = bf16[8,64,32]{2,1,0:T(8,128)(2,1)S(1)} fusion(f32[8,64,128]{2,1,0:T(8,128)S(1)} %bitcast.31, s32[8,64,32]{2,1,0:T(8,128)S(1)} %broadcast_add_fusion.1), kind=kLoop, calls=%fused_computation.9 | loop fusion | flops 6275072 | bytes 360448 | tf_op jit(solution)/shard_map/reduce_sum | solution.py:52
  56.7 0.2 convert_element_type.73
  56.9 11.1 %all_gather.6 = bf16[4,8,2048]{2,1,0:T(8,128)(2,1)S(1)} all-gather(bf16[1,8,2048]{2,1,0:T(8,128)(2,1)S(1)} %convert_element_type.73), channel_id=1, replica_groups=mesh['site'=4,'dev'=8] {'site'}, dimensions={0}, use_global_device_ids=true | all-gather | bytes 163840 | tf_op jit(solution)/shard_map/all_gather | solution.py:55
  68.0 29.3 %while.14 = (s32[]{:T(128)}, f32[8,64,128]{2,1,0:T(8,128)S(1)}, s32[4,8,128,16]{2,3,1,0:T(8,128)}, bf16[4,8,2048]{2,1,0:T(8,128)(2,1)S(1)}, s32[]{:T(128)}, /*index=5*/s32[]{:T(128)}) while((s32[]{:T(128)}, f32[8,64,128]{2,1,0:T(8,128)S(1)}, s32[4,8,128,16]{2,3,1,0:T(8,128)}, bf16[4,8,2048]{2,1,0:T(8,128)(2,1)S(1)}, s32[]{:T(128)}, ...), condition=%wide.region_4.5_spmd.clone, body=%wide.region_2.4_spmd.clone.sunk | while | flops 6389765 | bytes 1933927 | solution.py:64
  68.0 0.8 constant_dynamic-slice_fusion.3
  68.9 0.2 copy.15
  69.1 0.1 squeeze.21
  69.5 5.7 %select_reduce_fusion.3 = f32[8,64,128]{2,1,0:T(8,128)S(1)} fusion(f32[8,64,32]{2,1,0:T(8,128)S(1)} %reshape.142, s32[8,64,32]{2,1,0:T(8,128)S(1)} %broadcast_add_fusion.3), kind=kLoop, calls=%fused_computation.2.clone.1 | loop fusion | flops 6225920 | bytes 393216 | tf_op jit(solution)/shard_map/while/body/eval_jaxpr/reduce_sum | solution.py:62
  75.4 0.8 constant_dynamic-slice_fusion.3
  76.2 0.2 copy.15
  76.9 5.7 %select_reduce_fusion.3 = f32[8,64,128]{2,1,0:T(8,128)S(1)} fusion(f32[8,64,32]{2,1,0:T(8,128)S(1)} %reshape.142, s32[8,64,32]{2,1,0:T(8,128)S(1)} %broadcast_add_fusion.3), kind=kLoop, calls=%fused_computation.2.clone.1 | loop fusion | flops 6225920 | bytes 393216 | tf_op jit(solution)/shard_map/while/body/eval_jaxpr/reduce_sum | solution.py:62
  82.7 0.8 constant_dynamic-slice_fusion.3
  83.5 0.2 copy.15
  84.2 5.7 %select_reduce_fusion.3 = f32[8,64,128]{2,1,0:T(8,128)S(1)} fusion(f32[8,64,32]{2,1,0:T(8,128)S(1)} %reshape.142, s32[8,64,32]{2,1,0:T(8,128)S(1)} %broadcast_add_fusion.3), kind=kLoop, calls=%fused_computation.2.clone.1 | loop fusion | flops 6225920 | bytes 393216 | tf_op jit(solution)/shard_map/while/body/eval_jaxpr/reduce_sum | solution.py:62
  90.0 0.8 constant_dynamic-slice_fusion.3
  90.9 0.2 copy.15
  91.5 5.7 %select_reduce_fusion.3 = f32[8,64,128]{2,1,0:T(8,128)S(1)} fusion(f32[8,64,32]{2,1,0:T(8,128)S(1)} %reshape.142, s32[8,64,32]{2,1,0:T(8,128)S(1)} %broadcast_add_fusion.3), kind=kLoop, calls=%fused_computation.2.clone.1 | loop fusion | flops 6225920 | bytes 393216 | tf_op jit(solution)/shard_map/while/body/eval_jaxpr/reduce_sum | solution.py:62
  97.4 0.7 convolution_multiply_fusion
  98.1 1.6 %subtract_convert_fusion = bf16[8,8192]{1,0:T(8,128)(2,1)} fusion(f32[8,8192]{1,0:T(8,128)S(1)} %mul.133, bf16[8,8192]{1,0:T(8,128)(2,1)} %param.9), kind=kLoop, calls=%fused_computation.22 | loop fusion | flops 196608 | bytes 524288 | tf_op jit(solution)/shard_map/convert_element_type | solution.py:67
  99.7 1.7 %fusion.12 = f32[512,128]{1,0:T(8,128)S(1)} fusion(pred[512,128]{1,0:T(8,128)(4,1)} %bitcast.32, f32[512,128]{1,0:T(8,128)} %copy-done.1, f32[128]{0:T(128)S(1)} %fusion.41, f32[128]{0:T(128)S(1)} %get-tuple-element.135, f32[128]{0:T(128)S(1)} %get-tuple-element.134, s32[128]{0:T(128)S(1)} %and_select_fusion.1), kind=kOutput, calls=%fused_computation.20 | convolution fusion | flops 100810752 | bytes 591872 | tf_op jit(solution)/shard_map/dot_general | solution.py:49
  101.4 0.7 subtract_bitcast_fusion
  102.1 24.3 %all-gather.2.cloned.1.call-done = bf16[64,8192]{1,0:T(8,128)(2,1)} async-done(((bf16[8,8192]{1,0:T(8,128)(2,1)}), bf16[64,8192]{1,0:T(8,128)(2,1)}) %all-gather.2.cloned.1.call-update) | async-done | bytes 1048592 | tf_op jit(solution)/shard_map/all_gather | solution.py:70
  126.4 2.7 %fusion.9 = bf16[1,128,64]{1,2,0:T(8,128)(2,1)} fusion(bf16[64,8192]{1,0:T(8,128)(2,1)} %all-gather.2.cloned.1.call-done, bf16[1,128,8192]{2,1,0:T(8,128)(2,1)S(1)} %copy-done), kind=kOutput, calls=%fused_computation.17 | convolution fusion | flops 134225920 | bytes 3162112 | tf_op jit(solution)/shard_map/dot_general | solution.py:68
  (51 shorter events, 2.6 us)
Async XLA Ops:
  7.2 1.6 %copy-start = (bf16[1,128,8192]{2,1,0:T(8,128)(2,1)S(1)}, bf16[1,128,8192]{2,1,0:T(8,128)(2,1)}, u32[]{:S(2)}) copy-start(bf16[1,128,8192]{2,1,0:T(8,128)(2,1)} %param.7) | copy-start | bytes 6291460
  7.2 42.0 %reduce-scatter.2.cloned.1.call-start = ((), (), s32[]{:S(2)}) async-start(), calls=%async_computation.1 | async-start | bytes 1179648 | tf_op jit(solution)/shard_map/reduce_scatter | solution.py:30
  10.9 38.3 %copy-start.2 = (f32[1,8,8192]{2,1,0:T(8,128)S(1)}, f32[1,8,8192]{2,1,0:T(8,128)}, u32[]{:S(2)}) copy-start(f32[1,8,8192]{2,1,0:T(8,128)} %param.10) | copy-start | bytes 786436
  10.9 115.5 %all-gather.2.cloned.1.call-start = ((), (), s32[]{:S(2)}) async-start(), calls=%async_computation.2 | async-start | bytes 1179648 | tf_op jit(solution)/shard_map/all_gather | solution.py:70
  50.9 0.7 copy-start.1
Sparse Core Ops, SparseCore 0:
  11.2 37.9 reduce-scatter.1
  99.8 26.5 all-gather.1
where the time goes:
time: 137 us; the launch traced here: 136 us
  waiting for transfers between devices  57.6 us (42%)
  other arithmetic  35.3 us (26%)
  between operations  14.2 us (10%)
  blocking collectives  11.1 us (8%)
  local copies, waits for them, and re-layouts  9.7 us (7%)
  matrix products  7.8 us (6%)
    reduce_scatter x1, waiting for transfers between devices, shards(): lax.psum_scatter(lax.dot_general(local_cotan, local_tokens, (((0,), (0,))...  33.2 us
    all_gather x1, waiting for transfers between devices, shards(): lax.all_gather(new_weight, 'dev', axis=0, tiled=True)  24.3 us
    reduce_sum x4, other arithmetic, add_site(): return running + jnp.sum(placed, axis=2)  22.8 us
    all_gather x1, blocking collectives, shards(): lax.all_gather(kept_values.reshape(1, row_total, -1), 'site', axis=0, til...  11.1 us
    reduce_sum x1, other arithmetic, shards(): jnp.sum(jnp.where(matches, coefs[:, :, None, :], 0.0), axis=3)  5.12 us
    dynamic_slice x8, local copies, waits for them, and re-layouts, add_site(): lanes_here = spread_index(kept_index[site_step])  4.16 us
    reduce_or x1, other arithmetic, shards(): jnp.any(own_lanes[..., None] == lane_iota, axis=2).astype(jnp.float32)  3.6 us
  transfers between devices with their start and end apart: 2, of which 2 were waited for; matrix products, arithmetic and copies ran while one was open for 5% of the time, Pallas kernels for 0%

commit v1 on v0

v1 whole, which is shorter than its diff:
```python
import functools

import jax
import jax.numpy as jnp
import ml_dtypes
import numpy as np
from jax import lax
from jax.experimental import pallas as pl
from jax.experimental.pallas import tpu as pltpu
from jax.sharding import PartitionSpec as P

momentum_decay = 0.999
step_size = 0.01
SPAN = 64
LANES = 128
CHUNKS = 4
MESH = pl.DeviceIdType.MESH
f32 = jnp.float32
bf16 = jnp.bfloat16


def split_table(table):
    high = table.astype(ml_dtypes.bfloat16)
    low = (table - high.astype(np.float64)).astype(ml_dtypes.bfloat16)
    return np.concatenate([high, high, low], axis=0)


def pair_tables():
    freq = np.arange(SPAN)[:, None]
    place = np.arange(SPAN)[None, :]
    factor = np.where(freq == 0, np.sqrt(1.0 / SPAN), np.sqrt(2.0 / SPAN))
    one = factor * np.cos(np.pi * (2 * place + 1) * freq / (2 * SPAN))
    pair = np.kron(np.eye(LANES // SPAN), one)
    return split_table(pair.T), split_table(pair)


def split_dot(field, factor):
    high = field.astype(bf16)
    low = (field - high.astype(f32)).astype(bf16)
    return jnp.dot(jnp.concatenate([high, low, high], axis=1), factor, preferred_element_type=f32)


def stack(field):
    return jnp.concatenate(
        [field[:, t * LANES:(t + 1) * LANES] for t in range(field.shape[1] // LANES)], axis=0
    )


def unstack(field, rows):
    return jnp.concatenate(
        [field[t * rows:(t + 1) * rows] for t in range(field.shape[0] // rows)], axis=1
    )


def flip_bits(index, bits):
    for power in range(bits.bit_length()):
        if (bits >> power) & 1:
            one = 1 << power
            index = index + one - 2 * one * ((index // one) % 2)
    return index


def kernel(
    n_dev, n_site,
    tok_hbm, cotan, weight, mom_hbm, index_hbm, forward, inverse,
    score_out, mom_out_hbm,
    tok, mom, index, mask, mom_new, terms, from_mate, chip_sum, from_chip, sent, from_site, new_rows,
    tok_sem, mom_sem, index_sem, out_sem,
    mate_send, mate_recv, chip_send, chip_recv, site_send, site_recv,
    row_send, row_recv, pass_send, pass_recv,
):
    chips = n_dev // 2
    rows, width = mom.shape
    span = width // CHUNKS
    tiles = span // LANES
    me = lax.axis_index("dev")
    site = lax.axis_index("site")
    chip, core = me // 2, me % 2
    mate = chip * 2 + 1 - core
    order = range(chips - 1, 0, -1)

    def peer(k):
        return flip_bits(chip, k) * 2 + core

    def other_site(k):
        return (site + k) % n_site

    barrier = pltpu.get_barrier_semaphore()
    pl.semaphore_signal(barrier, inc=1, device_id={"dev": mate}, device_id_type=MESH)
    for k in order:
        pl.semaphore_signal(barrier, inc=1, device_id={"dev": peer(k)}, device_id_type=MESH)
    for k in range(1, n_site):
        pl.semaphore_signal(barrier, inc=1, device_id={"site": other_site(k)}, device_id_type=MESH)

    def cols(q):
        return slice(q * span, (q + 1) * span)

    tok_loads = [
        pltpu.make_async_copy(tok_hbm.at[0, :, cols(q)], tok.at[:, cols(q)], tok_sem.at[q])
        for q in range(CHUNKS)
    ]
    for load in tok_loads:
        load.start()
    index_load = pltpu.make_async_copy(index_hbm.at[site], index, index_sem)
    index_load.start()
    mom_load = pltpu.make_async_copy(mom_hbm.at[0], mom, mom_sem)
    mom_load.start()

    def remote(src, dst, send_sem, recv_sem, **where):
        return pltpu.make_async_remote_copy(
            src_ref=src, dst_ref=dst, send_sem=send_sem, recv_sem=recv_sem,
            device_id=where, device_id_type=MESH,
        )

    def mate_copy(q):
        return remote(
            terms.at[1 - core, q], from_mate.at[q], mate_send.at[q], mate_recv.at[q], dev=mate
        )

    def chip_copy(q, k):
        return remote(
            chip_sum.at[q, flip_bits(chip, k)], from_chip.at[q, k - 1],
            chip_send.at[q, k - 1], chip_recv.at[q, k - 1], dev=peer(k),
        )

    def site_copy(q, k):
        return remote(
            sent.at[q], from_site.at[q, k - 1],
            site_send.at[q, k - 1], site_recv.at[q, k - 1], site=other_site(k),
        )

    def row_copy(q, k):
        to = mate if k == 0 else peer(k)
        return remote(
            new_rows.at[q, me], new_rows.at[q, me], row_send.at[q, k], row_recv.at[q, k], dev=to
        )

    def row_arrival(q, k):
        held = new_rows.at[q, mate if k == 0 else peer(k)]
        return remote(held, held, row_send.at[q, k], row_recv.at[q, k], dev=mate)

    def pass_copy(q, k):
        held = new_rows.at[q, peer(k)]
        return remote(held, held, pass_send.at[q, k - 1], pass_recv.at[q, k - 1], dev=mate)

    def pass_arrival(q, k):
        held = new_rows.at[q, flip_bits(chip, k) * 2 + 1 - core]
        return remote(held, held, pass_send.at[q, k - 1], pass_recv.at[q, k - 1], dev=mate)

    def multiply(q):
        tok_loads[q].wait()
        grad = jnp.dot(cotan[...], tok[:, cols(q)], preferred_element_type=f32)
        grad = grad.reshape(chips, 2, rows, span)
        for c in range(2):
            part = grad[:, c]
            part = jnp.concatenate(
                [part[:, :, t * LANES:(t + 1) * LANES] for t in range(tiles)], axis=1
            )
            terms[c, q] = part.astype(bf16)
        if q == 0:
            pl.semaphore_wait(barrier, chips + n_site - 1)
        mate_copy(q).start()

    def add_mate(q):
        mate_copy(q).wait_recv()
        both = terms[core, q].astype(f32) + from_mate[q].astype(f32)
        chip_sum[q] = both.astype(bf16)
        for k in order:
            chip_copy(q, k).start()

    def make_mask():
        index_load.wait()
        held = index[...]
        one = jnp.int32(1)
        low = jnp.sum(jnp.where(held < 32, one << (held & 31), 0), axis=1)
        high = jnp.sum(jnp.where(held >= 32, one << (held & 31), 0), axis=1)
        lane = lax.broadcasted_iota(jnp.int32, (rows, LANES), 1)
        first = lane < SPAN
        lower = (lane % SPAN) < 32
        shift = lane % 32
        for t in range(width // LANES):
            def word(block):
                return jnp.where(
                    lower,
                    jnp.broadcast_to(low[:, block:block + 1], (rows, LANES)),
                    jnp.broadcast_to(high[:, block:block + 1], (rows, LANES)),
                )
            words = jnp.where(first, word(2 * t), word(2 * t + 1))
            mask[t * rows:(t + 1) * rows, :] = ((words >> shift) & 1).astype(f32)

    def pick(q):
        if q == 0:
            mom_load.wait()
        for k in order:
            chip_copy(q, k).wait_recv()
        grad = terms[core, q, chip].astype(f32) + from_mate[q, chip].astype(f32)
        for k in order:
            grad = grad + from_chip[q, k - 1].astype(f32)
        raised = momentum_decay * stack(mom[:, cols(q)]) + grad
        picked = split_dot(raised, forward[...]) * mask[q * tiles * rows:(q + 1) * tiles * rows, :]
        sent[q] = picked.astype(bf16)
        for k in range(1, n_site):
            site_copy(q, k).start()
        kept = raised - split_dot(picked, inverse[...])
        mom_new[:, cols(q)] = unstack(kept, rows)
        mom_store(q).start()

    def mom_store(q):
        return pltpu.make_async_copy(
            mom_new.at[:, cols(q)], mom_out_hbm.at[0, :, cols(q)], out_sem.at[q]
        )

    def update(q):
        for k in range(1, n_site):
            site_copy(q, k).wait_recv()
        total = sent[q].astype(f32)
        for k in range(1, n_site):
            total = total + from_site[q, k - 1].astype(f32)
        decoded = split_dot(total, inverse[...])
        new_rows[q, me] = (
            stack(weight[:, cols(q)].astype(f32)) - step_size * decoded
        ).astype(bf16)
        for k in order:
            row_copy(q, k).start()
        row_copy(q, 0).start()

    def hand_on(q):
        for k in range(1, chips):
            row_arrival(q, k).wait_recv()
            pass_copy(q, k).start()

    def project(q, scores):
        row_arrival(q, 0).wait_recv()
        for k in range(1, chips):
            pass_arrival(q, k).wait_recv()
        held = new_rows[q].astype(f32)
        held = jnp.concatenate(
            [held[:, t * rows:(t + 1) * rows, :].reshape(n_dev * rows, LANES) for t in range(tiles)],
            axis=1,
        ).astype(bf16)
        return scores + lax.dot_general(
            held, tok[:, cols(q)], (((1,), (1,)), ((), ())), preferred_element_type=f32
        )

    scores = jnp.zeros(score_out.shape[1:], f32)
    for step in range(CHUNKS + 5):
        if step == 2:
            make_mask()
        for stage, shift in ((multiply, 0), (add_mate, 1), (pick, 2), (update, 3), (hand_on, 4)):
            if 0 <= step - shift < CHUNKS:
                stage(step - shift)
        if 0 <= step - 5 < CHUNKS:
            scores = project(step - 5, scores)
    score_out[0] = scores.astype(bf16)

    for q in range(CHUNKS):
        mate_copy(q).wait_send()
        for k in range(1, chips):
            chip_copy(q, k).wait_send()
            row_copy(q, k).wait_send()
            pass_copy(q, k).wait_send()
        row_copy(q, 0).wait_send()
        for k in range(1, n_site):
            site_copy(q, k).wait_send()
        mom_store(q).wait()


def shards(n_dev, n_site, tokens, cotangent, weight, momentum, kept_index):
    count, width = tokens.shape[1:]
    out_rows = cotangent.shape[2]
    rows = weight.shape[0]
    chips = n_dev // 2
    high = rows * width // LANES // CHUNKS
    forward, inverse = pair_tables()
    vmem = pl.BlockSpec(memory_space=pltpu.VMEM)
    anywhere = pl.BlockSpec(memory_space=pl.ANY)
    sems = pltpu.SemaphoreType.DMA
    kept = kept_index.shape[3]
    scores, momentum_new = pl.pallas_call(
        functools.partial(kernel, n_dev, n_site),
        out_shape=(
            jax.ShapeDtypeStruct((1, out_rows, count), bf16),
            jax.ShapeDtypeStruct(momentum.shape, f32),
        ),
        in_specs=[anywhere, vmem, vmem, anywhere, anywhere, vmem, vmem],
        out_specs=(vmem, anywhere),
        scratch_shapes=[
            pltpu.VMEM((count, width), bf16),
            pltpu.VMEM((rows, width), f32),
            pltpu.VMEM((rows, kept, width // SPAN), jnp.int32),
            pltpu.VMEM((high * CHUNKS, LANES), f32),
            pltpu.VMEM((rows, width), f32),
            pltpu.VMEM((2, CHUNKS, chips, high, LANES), bf16),
            pltpu.VMEM((CHUNKS, chips, high, LANES), bf16),
            pltpu.VMEM((CHUNKS, chips, high, LANES), bf16),
            pltpu.VMEM((CHUNKS, chips - 1, high, LANES), bf16),
            pltpu.VMEM((CHUNKS, high, LANES), bf16),
            pltpu.VMEM((CHUNKS, n_site - 1, high, LANES), bf16),
            pltpu.VMEM((CHUNKS, n_dev, high, LANES), bf16),
            sems((CHUNKS,)), sems, sems, sems((CHUNKS,)),
            sems((CHUNKS,)), sems((CHUNKS,)),
            sems((CHUNKS, chips - 1)), sems((CHUNKS, chips - 1)),
            sems((CHUNKS, n_site - 1)), sems((CHUNKS, n_site - 1)),
            sems((CHUNKS, chips)), sems((CHUNKS, chips)),
            sems((CHUNKS, chips - 1)), sems((CHUNKS, chips - 1)),
        ],
        compiler_params=pltpu.CompilerParams(
            collective_id=0, has_side_effects=True, vmem_limit_bytes=50 * 1024 * 1024
        ),
        cost_estimate=pl.CostEstimate(
            flops=4 * count * width * out_rows, bytes_accessed=4 * count * width, transcendentals=0
        ),
    )(
        tokens,
        cotangent[0].T,
        weight,
        momentum,
        kept_index.transpose(0, 1, 3, 2),
        jnp.asarray(forward),
        jnp.asarray(inverse),
    )
    return scores.transpose(0, 2, 1), momentum_new


def solution(mesh):
    placed = (
        P("site", "dev", None),
        P("site", "dev", None),
        P("dev", None),
        P("site", "dev", None),
        P(None, "dev", None, None),
    )
    return jax.shard_map(
        functools.partial(shards, mesh.shape["dev"], mesh.shape["site"]),
        mesh=mesh,
        in_specs=placed,
        out_specs=(P("site", "dev", None), P("site", "dev", None)),
        check_vma=False,
    )
```

time: 137 us -> 39.1 us (0.29)
  waiting for transfers between devices: 57.6 us -> 0 us
  other arithmetic: 35.3 us -> 0 us
  Pallas kernels: 0 us -> 29.9 us
  between operations: 14.2 us -> 0.65 us
  blocking collectives: 11.1 us -> 0 us
  matrix products: 7.8 us -> 0 us
  local copies, waits for them, and re-layouts: 9.7 us -> 8.2 us
    reduce_scatter x1 -> x0, waiting for transfers between devices: 33.2 us -> none  [shards(): lax.psum_scatter(lax.dot_general(local_cotan, local_tokens, (((0,), (0,))...]
    pallas_call x0 -> x1, Pallas kernels: none -> 29.9 us  [shards(): pl.pallas_call(functools.partial(kernel, n_dev, n_site), out_shape=(jax.S...]
    reduce_sum x5 -> x0, other arithmetic: 27.9 us -> none  [the longest x4 22.8 us: add_site(): return running + jnp.sum(placed, axis=2)]
    all_gather x1 -> x0, waiting for transfers between devices: 24.3 us -> none  [shards(): lax.all_gather(new_weight, 'dev', axis=0, tiled=True)]
    all_gather x1 -> x0, blocking collectives: 11.1 us -> none  [shards(): lax.all_gather(kept_values.reshape(1, row_total, -1), 'site', axis=0, til...]
    dot_general x5 -> x0, matrix products: 7.8 us -> none  [the longest x1 2.67 us: shards(): lax.dot_general(local_tokens, lax.all_gather(new_weight, 'dev', axis=0, t...]
    unnamed x6 -> x16, local copies, waits for them, and re-layouts: 2.24 us -> 8.2 us
    dynamic_slice x10 -> x0, local copies, waits for them, and re-layouts: 5.21 us -> none  [the longest x8 4.16 us: add_site(): lanes_here = spread_index(kept_index[site_step])]
  transfers between devices with their start and end apart: 2 -> 0, of which waited for: 2 -> 0; matrix products, arithmetic and copies ran while one was open for 5% -> 0% of each run, Pallas kernels for 0% -> 0%
where the time goes in v1:
time: 39.1 us; the launch traced here: 38.8 us
  Pallas kernels  29.9 us (76%)
  local copies, waits for them, and re-layouts  8.2 us (21%)
  between operations  0.65 us (2%)
    pallas_call x1, Pallas kernels, shards(): pl.pallas_call(functools.partial(kernel, n_dev, n_site), out_shape=(jax.S...  29.9 us
    unnamed x16, local copies, waits for them, and re-layouts  8.2 us

profile of v1, /device:TPU:1, one launch (start us, length us, event | category | flops | bytes accessed | tf_op | source)
XLA Modules:
  0.0 38.8 jit_solution(1279458007367807648)
XLA Ops:
  0.6 0.0 copy-start
  0.6 1.6 %copy-done = bf16[1,128,8192]{2,1,0:T(8,128)(2,1)S(1)} copy-done((bf16[1,128,8192]{2,1,0:T(8,128)(2,1)S(1)}, bf16[1,128,8192]{2,1,0:T(8,128)(2,1)}, u32[]{:S(2)}) %copy-start) | copy-done | bytes 2097176
  2.2 0.0 copy-start.1
  2.2 0.9 %copy-done.1 = f32[1,8,8192]{2,1,0:T(8,128)S(1)} copy-done((f32[1,8,8192]{2,1,0:T(8,128)S(1)}, f32[1,8,8192]{2,1,0:T(8,128)}, u32[]{:S(2)}) %copy-start.1) | copy-done | bytes 262168
  3.2 0.0 copy-start.2
  3.2 0.9 %copy-done.2 = s32[4,8,128,16]{2,3,1,0:T(8,128)S(1)} copy-done((s32[4,8,128,16]{2,3,1,0:T(8,128)S(1)}, s32[4,8,128,16]{2,3,1,0:T(8,128)}, u32[]{:S(2)}) %copy-start.2) | copy-done | bytes 262168
  4.1 0.0 copy-start.3
  4.1 0.9 %copy-done.3 = bf16[8,8192]{1,0:T(8,128)(2,1)S(1)} copy-done((bf16[8,8192]{1,0:T(8,128)(2,1)S(1)}, bf16[8,8192]{1,0:T(8,128)(2,1)}, u32[]{:S(2)}) %copy-start.3) | copy-done | bytes 131096
  5.0 0.0 copy-start.4
  5.0 0.9 %copy-done.4 = bf16[384,128]{1,0:T(8,128)(2,1)S(1)} copy-done((bf16[384,128]{1,0:T(8,128)(2,1)S(1)}, bf16[384,128]{1,0:T(8,128)(2,1)}, u32[]{:S(2)}) %copy-start.4) | copy-done | bytes 98328
  5.9 0.0 copy-start.5
  5.9 0.9 %copy-done.5 = bf16[384,128]{1,0:T(8,128)(2,1)S(1)} copy-done((bf16[384,128]{1,0:T(8,128)(2,1)S(1)}, bf16[384,128]{1,0:T(8,128)(2,1)}, u32[]{:S(2)}) %copy-start.5) | copy-done | bytes 98328
  6.8 0.0 copy-start.6
  6.8 0.7 %copy-done.6 = bf16[1,128,64]{1,2,0:T(8,128)(2,1)S(1)} copy-done((bf16[1,128,64]{1,2,0:T(8,128)(2,1)S(1)}, bf16[1,128,64]{1,2,0:T(8,128)(2,1)}, u32[]{:S(2)}) %copy-start.6) | copy-done | bytes 16408
  7.5 29.9 %shard_map.86 = (bf16[1,64,128]{2,1,0:T(8,128)(2,1)S(1)}, f32[1,8,8192]{2,1,0:T(8,128)S(1)}) custom-call(bf16[1,128,8192]{2,1,0:T(8,128)(2,1)S(1)} %copy-done, bf16[64,128]{1,0:T(8,128)(2,1)S(1)} %bitcast.6, bf16[8,8192]{1,0:T(8,128)(2,1)S(1)} %copy-done.3, f32[1,8,8192]{2,1,0:T(8,128)S(1)} %copy-done.1, s32[4,8,16,128]{3,2,1,0:T(8,128)S(1)} %bitcast.5, ...), custom_call_target="tpu_custom_call" | custom-call | flops 268435456 | bytes 4194304 | tf_op jit(solution)/shard_map/pallas_call | solution.py:279
  37.5 0.6 %copy.11 = bf16[1,128,64]{1,2,0:T(8,128)(2,1)} copy(bf16[1,128,64]{1,2,0:T(8,128)(2,1)S(1)} %bitcast.7) | data formatting | bytes 32768
  38.1 0.7 %copy.12 = f32[1,8,8192]{2,1,0:T(8,128)} copy(f32[1,8,8192]{2,1,0:T(8,128)S(1)} %get-tuple-element.9) | data formatting | bytes 524288
Async XLA Ops:
  0.6 1.6 %copy-start = (bf16[1,128,8192]{2,1,0:T(8,128)(2,1)S(1)}, bf16[1,128,8192]{2,1,0:T(8,128)(2,1)}, u32[]{:S(2)}) copy-start(bf16[1,128,8192]{2,1,0:T(8,128)(2,1)} %tok_hbm.1) | copy-start | bytes 6291460
  2.2 0.9 %copy-start.1 = (f32[1,8,8192]{2,1,0:T(8,128)S(1)}, f32[1,8,8192]{2,1,0:T(8,128)}, u32[]{:S(2)}) copy-start(f32[1,8,8192]{2,1,0:T(8,128)} %mom_hbm.1) | copy-start | bytes 786436
  3.2 0.9 %copy-start.2 = (s32[4,8,128,16]{2,3,1,0:T(8,128)S(1)}, s32[4,8,128,16]{2,3,1,0:T(8,128)}, u32[]{:S(2)}) copy-start(s32[4,8,128,16]{2,3,1,0:T(8,128)} %param.11) | copy-start | bytes 786436
  4.1 0.9 %copy-start.3 = (bf16[8,8192]{1,0:T(8,128)(2,1)S(1)}, bf16[8,8192]{1,0:T(8,128)(2,1)}, u32[]{:S(2)}) copy-start(bf16[8,8192]{1,0:T(8,128)(2,1)} %weight.1) | copy-start | bytes 393220
  5.0 0.9 %copy-start.4 = (bf16[384,128]{1,0:T(8,128)(2,1)S(1)}, bf16[384,128]{1,0:T(8,128)(2,1)}, u32[]{:S(2)}) copy-start(bf16[384,128]{1,0:T(8,128)(2,1)} %constant.5.clone.inverse) | copy-start | bytes 294916
  5.9 0.9 %copy-start.5 = (bf16[384,128]{1,0:T(8,128)(2,1)S(1)}, bf16[384,128]{1,0:T(8,128)(2,1)}, u32[]{:S(2)}) copy-start(bf16[384,128]{1,0:T(8,128)(2,1)} %constant.4.clone.forward) | copy-start | bytes 294916
  6.8 0.7 %copy-start.6 = (bf16[1,128,64]{1,2,0:T(8,128)(2,1)S(1)}, bf16[1,128,64]{1,2,0:T(8,128)(2,1)}, u32[]{:S(2)}) copy-start(bf16[1,128,64]{1,2,0:T(8,128)(2,1)} %param.8) | copy-start | bytes 49156

commit v2 on v1

--- a/solution.py
+++ b/solution.py
@@ -31,7 +31,7 @@
     factor = np.where(freq == 0, np.sqrt(1.0 / SPAN), np.sqrt(2.0 / SPAN))
     one = factor * np.cos(np.pi * (2 * place + 1) * freq / (2 * SPAN))
     pair = np.kron(np.eye(LANES // SPAN), one)
-    return split_table(pair.T), split_table(pair)
+    return np.stack([split_table(pair.T), split_table(pair)])
 
 
 def split_dot(field, factor):
@@ -62,10 +62,10 @@
 
 def kernel(
     n_dev, n_site,
-    tok_hbm, cotan, weight, mom_hbm, index_hbm, forward, inverse,
+    tok_hbm, cotan_hbm, weight_hbm, mom_hbm, index_hbm, table_hbm,
     score_out, mom_out_hbm,
-    tok, mom, index, mask, mom_new, terms, from_mate, chip_sum, from_chip, sent, from_site, new_rows,
-    tok_sem, mom_sem, index_sem, out_sem,
+    cotan, weight, table, tok, mom, index, mask, mom_new, terms, from_mate, chip_sum, from_chip, sent, from_site, new_rows,
+    cotan_sem, weight_sem, table_sem, tok_sem, mom_sem, index_sem, out_sem,
     mate_send, mate_recv, chip_send, chip_recv, site_send, site_recv,
     row_send, row_recv, pass_send, pass_recv,
 ):
@@ -99,12 +99,18 @@
         pltpu.make_async_copy(tok_hbm.at[0, :, cols(q)], tok.at[:, cols(q)], tok_sem.at[q])
         for q in range(CHUNKS)
     ]
+    cotan_load = pltpu.make_async_copy(cotan_hbm, cotan, cotan_sem)
+    weight_load = pltpu.make_async_copy(weight_hbm, weight, weight_sem)
+    table_load = pltpu.make_async_copy(table_hbm, table, table_sem)
+    cotan_load.start()
     for load in tok_loads:
         load.start()
     index_load = pltpu.make_async_copy(index_hbm.at[site], index, index_sem)
     index_load.start()
     mom_load = pltpu.make_async_copy(mom_hbm.at[0], mom, mom_sem)
     mom_load.start()
+    table_load.start()
+    weight_load.start()
 
     def remote(src, dst, send_sem, recv_sem, **where):
         return pltpu.make_async_remote_copy(
@@ -148,6 +154,8 @@
         return remote(held, held, pass_send.at[q, k - 1], pass_recv.at[q, k - 1], dev=mate)
 
     def multiply(q):
+        if q == 0:
+            cotan_load.wait()
         tok_loads[q].wait()
         grad = jnp.dot(cotan[...], tok[:, cols(q)], preferred_element_type=f32)
         grad = grad.reshape(chips, 2, rows, span)
@@ -191,17 +199,18 @@
     def pick(q):
         if q == 0:
             mom_load.wait()
+            table_load.wait()
         for k in order:
             chip_copy(q, k).wait_recv()
         grad = terms[core, q, chip].astype(f32) + from_mate[q, chip].astype(f32)
         for k in order:
             grad = grad + from_chip[q, k - 1].astype(f32)
         raised = momentum_decay * stack(mom[:, cols(q)]) + grad
-        picked = split_dot(raised, forward[...]) * mask[q * tiles * rows:(q + 1) * tiles * rows, :]
+        picked = split_dot(raised, table[0]) * mask[q * tiles * rows:(q + 1) * tiles * rows, :]
         sent[q] = picked.astype(bf16)
         for k in range(1, n_site):
             site_copy(q, k).start()
-        kept = raised - split_dot(picked, inverse[...])
+        kept = raised - split_dot(picked, table[1])
         mom_new[:, cols(q)] = unstack(kept, rows)
         mom_store(q).start()
 
@@ -213,10 +222,12 @@
     def update(q):
         for k in range(1, n_site):
             site_copy(q, k).wait_recv()
+        if q == 0:
+            weight_load.wait()
         total = sent[q].astype(f32)
         for k in range(1, n_site):
             total = total + from_site[q, k - 1].astype(f32)
-        decoded = split_dot(total, inverse[...])
+        decoded = split_dot(total, table[1])
         new_rows[q, me] = (
             stack(weight[:, cols(q)].astype(f32)) - step_size * decoded
         ).astype(bf16)
@@ -243,10 +254,15 @@
         )
 
     scores = jnp.zeros(score_out.shape[1:], f32)
+    for q in range(CHUNKS):
+        multiply(q)
+    for q in range(CHUNKS):
+        add_mate(q)
+    make_mask()
     for step in range(CHUNKS + 5):
-        if step == 2:
-            make_mask()
-        for stage, shift in ((multiply, 0), (add_mate, 1), (pick, 2), (update, 3), (hand_on, 4)):
+        if step < CHUNKS:
+            pick(step)
+        for stage, shift in ((update, 2), (hand_on, 4)):
             if 0 <= step - shift < CHUNKS:
                 stage(step - shift)
         if 0 <= step - 5 < CHUNKS:
@@ -271,9 +287,9 @@
     rows = weight.shape[0]
     chips = n_dev // 2
     high = rows * width // LANES // CHUNKS
-    forward, inverse = pair_tables()
+    tables = pair_tables()
     vmem = pl.BlockSpec(memory_space=pltpu.VMEM)
-    anywhere = pl.BlockSpec(memory_space=pl.ANY)
+    hbm = pl.BlockSpec(memory_space=pltpu.HBM)
     sems = pltpu.SemaphoreType.DMA
     kept = kept_index.shape[3]
     scores, momentum_new = pl.pallas_call(
@@ -282,9 +298,12 @@
             jax.ShapeDtypeStruct((1, out_rows, count), bf16),
             jax.ShapeDtypeStruct(momentum.shape, f32),
         ),
-        in_specs=[anywhere, vmem, vmem, anywhere, anywhere, vmem, vmem],
-        out_specs=(vmem, anywhere),
+        in_specs=[hbm] * 6,
+        out_specs=(vmem, hbm),
         scratch_shapes=[
+            pltpu.VMEM((out_rows, count), bf16),
+            pltpu.VMEM((rows, width), bf16),
+            pltpu.VMEM(tables.shape, bf16),
             pltpu.VMEM((count, width), bf16),
             pltpu.VMEM((rows, width), f32),
             pltpu.VMEM((rows, kept, width // SPAN), jnp.int32),
@@ -297,7 +316,7 @@
             pltpu.VMEM((CHUNKS, high, LANES), bf16),
             pltpu.VMEM((CHUNKS, n_site - 1, high, LANES), bf16),
             pltpu.VMEM((CHUNKS, n_dev, high, LANES), bf16),
-            sems((CHUNKS,)), sems, sems, sems((CHUNKS,)),
+            sems, sems, sems, sems((CHUNKS,)), sems, sems, sems((CHUNKS,)),
             sems((CHUNKS,)), sems((CHUNKS,)),
             sems((CHUNKS, chips - 1)), sems((CHUNKS, chips - 1)),
             sems((CHUNKS, n_site - 1)), sems((CHUNKS, n_site - 1)),
@@ -305,7 +324,7 @@
             sems((CHUNKS, chips - 1)), sems((CHUNKS, chips - 1)),
         ],
         compiler_params=pltpu.CompilerParams(
-            collective_id=0, has_side_effects=True, vmem_limit_bytes=50 * 1024 * 1024
+            collective_id=0, has_side_effects=True, vmem_limit_bytes=56 * 1024 * 1024
         ),
         cost_estimate=pl.CostEstimate(
             flops=4 * count * width * out_rows, bytes_accessed=4 * count * width, transcendentals=0
@@ -316,8 +335,7 @@
         weight,
         momentum,
         kept_index.transpose(0, 1, 3, 2),
-        jnp.asarray(forward),
-        jnp.asarray(inverse),
+        jnp.asarray(tables),
     )
     return scores.transpose(0, 2, 1), momentum_new
 

time: 39.1 us -> 33.7 us (0.86)
  local copies, waits for them, and re-layouts: 8.2 us -> 2.99 us
    unnamed x16 -> x2, local copies, waits for them, and re-layouts: 8.2 us -> 2.99 us
where the time goes in v2:
time: 33.7 us; the launch traced here: 33.5 us
  Pallas kernels  29.8 us (88%)
  local copies, waits for them, and re-layouts  2.99 us (9%)
  between operations  0.64 us (2%)
    pallas_call x1, Pallas kernels, shards(): pl.pallas_call(functools.partial(kernel, n_dev, n_site), out_shape=(jax.S...  29.8 us
    unnamed x2, local copies, waits for them, and re-layouts  2.99 us

profile of v2, /device:TPU:1, one launch (start us, length us, event | category | flops | bytes accessed | tf_op | source)
XLA Modules:
  0.0 33.5 jit_solution(11625736850119336937)
XLA Ops:
  0.6 29.8 %shard_map.77 = (bf16[1,64,128]{2,1,0:T(8,128)(2,1)}, f32[1,8,8192]{2,1,0:T(8,128)}) custom-call(bf16[1,128,8192]{2,1,0:T(8,128)(2,1)} %tok_hbm.1, bf16[64,128]{1,0:T(8,128)(2,1)} %bitcast.6, bf16[8,8192]{1,0:T(8,128)(2,1)} %weight_hbm.1, f32[1,8,8192]{2,1,0:T(8,128)} %mom_hbm.1, s32[4,8,16,128]{3,2,1,0:T(8,128)} %bitcast.5, ...), custom_call_target="tpu_custom_call" | custom-call | flops 268435456 | bytes 4194304 | tf_op jit(solution)/shard_map/pallas_call | solution.py:295
  30.5 1.3 %copy.10 = bf16[1,128,64]{1,2,0:T(8,128)(2,1)} copy(bf16[1,128,64]{1,2,0:T(8,128)(2,1)} %bitcast.7) | data formatting | bytes 32768
  31.8 1.7 %copy.11 = f32[1,8,8192]{2,1,0:T(8,128)} copy(f32[1,8,8192]{2,1,0:T(8,128)} %get-tuple-element.9) | data formatting | bytes 524288

commit v3 on v2

--- a/solution.py
+++ b/solution.py
@@ -13,7 +13,6 @@
 step_size = 0.01
 SPAN = 64
 LANES = 128
-CHUNKS = 4
 MESH = pl.DeviceIdType.MESH
 f32 = jnp.float32
 bf16 = jnp.bfloat16
@@ -61,18 +60,19 @@
 
 
 def kernel(
-    n_dev, n_site,
+    n_dev, n_site, chunks,
     tok_hbm, cotan_hbm, weight_hbm, mom_hbm, index_hbm, table_hbm,
-    score_out, mom_out_hbm,
-    cotan, weight, table, tok, mom, index, mask, mom_new, terms, from_mate, chip_sum, from_chip, sent, from_site, new_rows,
-    cotan_sem, weight_sem, table_sem, tok_sem, mom_sem, index_sem, out_sem,
-    mate_send, mate_recv, chip_send, chip_recv, site_send, site_recv,
+    score_out, mom_out,
+    cotan, weight, table, tok, mom, index, mask, terms, from_mate, chip_sum, from_chip, sent, from_site, new_rows,
+    cotan_sem, weight_sem, table_sem, tok_sem, mom_sem, index_sem,
+    mate_send, mate_recv, chip_send, chip_recv, site_send, site_recv, share_send, share_recv,
     row_send, row_recv, pass_send, pass_recv,
 ):
     chips = n_dev // 2
     rows, width = mom.shape
-    span = width // CHUNKS
+    span = width // chunks
     tiles = span // LANES
+    piece = tiles * rows // n_site
     me = lax.axis_index("dev")
     site = lax.axis_index("site")
     chip, core = me // 2, me % 2
@@ -92,12 +92,15 @@
     for k in range(1, n_site):
         pl.semaphore_signal(barrier, inc=1, device_id={"site": other_site(k)}, device_id_type=MESH)
 
+    def piece_of(index):
+        return pl.ds(pl.multiple_of(index * piece, piece), piece)
+
     def cols(q):
         return slice(q * span, (q + 1) * span)
 
     tok_loads = [
         pltpu.make_async_copy(tok_hbm.at[0, :, cols(q)], tok.at[:, cols(q)], tok_sem.at[q])
-        for q in range(CHUNKS)
+        for q in range(chunks)
     ]
     cotan_load = pltpu.make_async_copy(cotan_hbm, cotan, cotan_sem)
     weight_load = pltpu.make_async_copy(weight_hbm, weight, weight_sem)
@@ -131,8 +134,20 @@
 
     def site_copy(q, k):
         return remote(
-            sent.at[q], from_site.at[q, k - 1],
+            sent.at[q, piece_of(other_site(k))], from_site.at[q, k - 1],
             site_send.at[q, k - 1], site_recv.at[q, k - 1], site=other_site(k),
+        )
+
+    def share_copy(q, k):
+        held = new_rows.at[q, me, piece_of(site)]
+        return remote(
+            held, held, share_send.at[q, k - 1], share_recv.at[q, k - 1], site=other_site(k)
+        )
+
+    def share_arrival(q, k):
+        held = new_rows.at[q, me, piece_of((site + n_site - k) % n_site)]
+        return remote(
+            held, held, share_send.at[q, k - 1], share_recv.at[q, k - 1], site=other_site(k)
         )
 
     def row_copy(q, k):
@@ -211,26 +226,28 @@
         for k in range(1, n_site):
             site_copy(q, k).start()
         kept = raised - split_dot(picked, table[1])
-        mom_new[:, cols(q)] = unstack(kept, rows)
-        mom_store(q).start()
-
-    def mom_store(q):
-        return pltpu.make_async_copy(
-            mom_new.at[:, cols(q)], mom_out_hbm.at[0, :, cols(q)], out_sem.at[q]
-        )
+        mom_out[0, :, cols(q)] = unstack(kept, rows)
 
     def update(q):
         for k in range(1, n_site):
             site_copy(q, k).wait_recv()
         if q == 0:
             weight_load.wait()
-        total = sent[q].astype(f32)
+        total = sent[q, piece_of(site)].astype(f32)
         for k in range(1, n_site):
             total = total + from_site[q, k - 1].astype(f32)
         decoded = split_dot(total, table[1])
-        new_rows[q, me] = (
-            stack(weight[:, cols(q)].astype(f32)) - step_size * decoded
+        wide = span // n_site
+        own = weight[:, pl.ds(pl.multiple_of(q * span + site * wide, wide), wide)]
+        new_rows[q, me, piece_of(site)] = (
+            stack(own.astype(f32)) - step_size * decoded
         ).astype(bf16)
+        for k in range(1, n_site):
+            share_copy(q, k).start()
+
+    def spread(q):
+        for k in range(1, n_site):
+            share_arrival(q, k).wait_recv()
         for k in order:
             row_copy(q, k).start()
         row_copy(q, 0).start()
@@ -254,22 +271,22 @@
         )
 
     scores = jnp.zeros(score_out.shape[1:], f32)
-    for q in range(CHUNKS):
+    for q in range(chunks):
         multiply(q)
-    for q in range(CHUNKS):
+    for q in range(chunks):
         add_mate(q)
     make_mask()
-    for step in range(CHUNKS + 5):
-        if step < CHUNKS:
+    for step in range(chunks + 6):
+        if step < chunks:
             pick(step)
-        for stage, shift in ((update, 2), (hand_on, 4)):
-            if 0 <= step - shift < CHUNKS:
+        for stage, shift in ((update, 1), (spread, 2), (hand_on, 4)):
+            if 0 <= step - shift < chunks:
                 stage(step - shift)
-        if 0 <= step - 5 < CHUNKS:
+        if 0 <= step - 5 < chunks:
             scores = project(step - 5, scores)
     score_out[0] = scores.astype(bf16)
 
-    for q in range(CHUNKS):
+    for q in range(chunks):
         mate_copy(q).wait_send()
         for k in range(1, chips):
             chip_copy(q, k).wait_send()
@@ -278,7 +295,7 @@
         row_copy(q, 0).wait_send()
         for k in range(1, n_site):
             site_copy(q, k).wait_send()
-        mom_store(q).wait()
+            share_copy(q, k).wait_send()
 
 
 def shards(n_dev, n_site, tokens, cotangent, weight, momentum, kept_index):
@@ -286,20 +303,21 @@
     out_rows = cotangent.shape[2]
     rows = weight.shape[0]
     chips = n_dev // 2
-    high = rows * width // LANES // CHUNKS
+    chunks = min(4, rows * width // LANES // (16 * n_site))
+    high = rows * width // LANES // chunks
     tables = pair_tables()
     vmem = pl.BlockSpec(memory_space=pltpu.VMEM)
     hbm = pl.BlockSpec(memory_space=pltpu.HBM)
     sems = pltpu.SemaphoreType.DMA
     kept = kept_index.shape[3]
     scores, momentum_new = pl.pallas_call(
-        functools.partial(kernel, n_dev, n_site),
+        functools.partial(kernel, n_dev, n_site, chunks),
         out_shape=(
-            jax.ShapeDtypeStruct((1, out_rows, count), bf16),
-            jax.ShapeDtypeStruct(momentum.shape, f32),
+            pltpu.VMEM((1, out_rows, count), bf16),
+            pltpu.VMEM(momentum.shape, f32),
         ),
         in_specs=[hbm] * 6,
-        out_specs=(vmem, hbm),
+        out_specs=(vmem, vmem),
         scratch_shapes=[
             pltpu.VMEM((out_rows, count), bf16),
             pltpu.VMEM((rows, width), bf16),
@@ -307,21 +325,21 @@
             pltpu.VMEM((count, width), bf16),
             pltpu.VMEM((rows, width), f32),
             pltpu.VMEM((rows, kept, width // SPAN), jnp.int32),
-            pltpu.VMEM((high * CHUNKS, LANES), f32),
-            pltpu.VMEM((rows, width), f32),
-            pltpu.VMEM((2, CHUNKS, chips, high, LANES), bf16),
-            pltpu.VMEM((CHUNKS, chips, high, LANES), bf16),
-            pltpu.VMEM((CHUNKS, chips, high, LANES), bf16),
-            pltpu.VMEM((CHUNKS, chips - 1, high, LANES), bf16),
-            pltpu.VMEM((CHUNKS, high, LANES), bf16),
-            pltpu.VMEM((CHUNKS, n_site - 1, high, LANES), bf16),
-            pltpu.VMEM((CHUNKS, n_dev, high, LANES), bf16),
-            sems, sems, sems, sems((CHUNKS,)), sems, sems, sems((CHUNKS,)),
-            sems((CHUNKS,)), sems((CHUNKS,)),
-            sems((CHUNKS, chips - 1)), sems((CHUNKS, chips - 1)),
-            sems((CHUNKS, n_site - 1)), sems((CHUNKS, n_site - 1)),
-            sems((CHUNKS, chips)), sems((CHUNKS, chips)),
-            sems((CHUNKS, chips - 1)), sems((CHUNKS, chips - 1)),
+            pltpu.VMEM((high * chunks, LANES), f32),
+            pltpu.VMEM((2, chunks, chips, high, LANES), bf16),
+            pltpu.VMEM((chunks, chips, high, LANES), bf16),
+            pltpu.VMEM((chunks, chips, high, LANES), bf16),
+            pltpu.VMEM((chunks, chips - 1, high, LANES), bf16),
+            pltpu.VMEM((chunks, high, LANES), bf16),
+            pltpu.VMEM((chunks, n_site - 1, high // n_site, LANES), bf16),
+            pltpu.VMEM((chunks, n_dev, high, LANES), bf16),
+            sems, sems, sems, sems((chunks,)), sems, sems,
+            sems((chunks,)), sems((chunks,)),
+            sems((chunks, chips - 1)), sems((chunks, chips - 1)),
+            sems((chunks, n_site - 1)), sems((chunks, n_site - 1)),
+            sems((chunks, n_site - 1)), sems((chunks, n_site - 1)),
+            sems((chunks, chips)), sems((chunks, chips)),
+            sems((chunks, chips - 1)), sems((chunks, chips - 1)),
         ],
         compiler_params=pltpu.CompilerParams(
             collective_id=0, has_side_effects=True, vmem_limit_bytes=56 * 1024 * 1024

time: 33.7 us -> 34.2 us (1.015)
  Pallas kernels: 29.8 us -> 32.1 us
  local copies, waits for them, and re-layouts: 2.99 us -> 1.31 us
    pallas_call x1, Pallas kernels: 29.8 us -> 32.1 us  [shards(): pl.pallas_call(functools.partial(kernel, n_dev, n_site, chunks), out_shap...]
    unnamed x2, local copies, waits for them, and re-layouts: 2.99 us -> 1.31 us
where the time goes in v3:
time: 34.2 us; the launch traced here: 34.1 us
  Pallas kernels  32.1 us (94%)
  local copies, waits for them, and re-layouts  1.31 us (4%)
  between operations  0.64 us (2%)
    pallas_call x1, Pallas kernels, shards(): pl.pallas_call(functools.partial(kernel, n_dev, n_site, chunks), out_shap...  32.1 us
    unnamed x2, local copies, waits for them, and re-layouts  1.31 us

profile of v3, /device:TPU:1, one launch (start us, length us, event | category | flops | bytes accessed | tf_op | source)
XLA Modules:
  0.0 34.1 jit_solution(67372191950514062)
XLA Ops:
  0.6 32.1 %shard_map.77 = (bf16[1,64,128]{2,1,0:T(8,128)(2,1)S(1)}, f32[1,8,8192]{2,1,0:T(8,128)S(1)}) custom-call(bf16[1,128,8192]{2,1,0:T(8,128)(2,1)} %tok_hbm.1, bf16[64,128]{1,0:T(8,128)(2,1)} %bitcast.7, bf16[8,8192]{1,0:T(8,128)(2,1)} %weight_hbm.1, f32[1,8,8192]{2,1,0:T(8,128)} %mom_hbm.1, s32[4,8,16,128]{3,2,1,0:T(8,128)} %bitcast.6, ...), custom_call_target="tpu_custom_call" | custom-call | flops 268435456 | bytes 4194304 | tf_op jit(solution)/shard_map/pallas_call | solution.py:313
  32.7 0.6 %copy.10 = bf16[1,128,64]{1,2,0:T(8,128)(2,1)} copy(bf16[1,128,64]{1,2,0:T(8,128)(2,1)S(1)} %bitcast.5) | data formatting | bytes 32768
  33.4 0.7 %copy.11 = f32[1,8,8192]{2,1,0:T(8,128)} copy(f32[1,8,8192]{2,1,0:T(8,128)S(1)} %get-tuple-element.7) | data formatting | bytes 524288

commit v4 on v2

--- a/solution.py
+++ b/solution.py
@@ -63,9 +63,9 @@
 def kernel(
     n_dev, n_site,
     tok_hbm, cotan_hbm, weight_hbm, mom_hbm, index_hbm, table_hbm,
-    score_out, mom_out_hbm,
-    cotan, weight, table, tok, mom, index, mask, mom_new, terms, from_mate, chip_sum, from_chip, sent, from_site, new_rows,
-    cotan_sem, weight_sem, table_sem, tok_sem, mom_sem, index_sem, out_sem,
+    score_out, mom_out,
+    cotan, weight, table, tok, mom, index, mask, total_scores, terms, from_mate, chip_sum, from_chip, sent, from_site, new_rows,
+    cotan_sem, weight_sem, table_sem, tok_sem, mom_sem, index_sem,
     mate_send, mate_recv, chip_send, chip_recv, site_send, site_recv,
     row_send, row_recv, pass_send, pass_recv,
 ):
@@ -93,18 +93,17 @@
         pl.semaphore_signal(barrier, inc=1, device_id={"site": other_site(k)}, device_id_type=MESH)
 
     def cols(q):
-        return slice(q * span, (q + 1) * span)
-
-    tok_loads = [
-        pltpu.make_async_copy(tok_hbm.at[0, :, cols(q)], tok.at[:, cols(q)], tok_sem.at[q])
-        for q in range(CHUNKS)
-    ]
+        return pl.ds(pl.multiple_of(q * span, span), span)
+
+    def tok_load(q):
+        return pltpu.make_async_copy(tok_hbm.at[0, :, cols(q)], tok.at[:, cols(q)], tok_sem.at[q])
+
     cotan_load = pltpu.make_async_copy(cotan_hbm, cotan, cotan_sem)
     weight_load = pltpu.make_async_copy(weight_hbm, weight, weight_sem)
     table_load = pltpu.make_async_copy(table_hbm, table, table_sem)
     cotan_load.start()
-    for load in tok_loads:
-        load.start()
+    for q in range(CHUNKS):
+        tok_load(q).start()
     index_load = pltpu.make_async_copy(index_hbm.at[site], index, index_sem)
     index_load.start()
     mom_load = pltpu.make_async_copy(mom_hbm.at[0], mom, mom_sem)
@@ -154,9 +153,7 @@
         return remote(held, held, pass_send.at[q, k - 1], pass_recv.at[q, k - 1], dev=mate)
 
     def multiply(q):
-        if q == 0:
-            cotan_load.wait()
-        tok_loads[q].wait()
+        tok_load(q).wait()
         grad = jnp.dot(cotan[...], tok[:, cols(q)], preferred_element_type=f32)
         grad = grad.reshape(chips, 2, rows, span)
         for c in range(2):
@@ -165,8 +162,6 @@
                 [part[:, :, t * LANES:(t + 1) * LANES] for t in range(tiles)], axis=1
             )
             terms[c, q] = part.astype(bf16)
-        if q == 0:
-            pl.semaphore_wait(barrier, chips + n_site - 1)
         mate_copy(q).start()
 
     def add_mate(q):
@@ -197,33 +192,22 @@
             mask[t * rows:(t + 1) * rows, :] = ((words >> shift) & 1).astype(f32)
 
     def pick(q):
-        if q == 0:
-            mom_load.wait()
-            table_load.wait()
         for k in order:
             chip_copy(q, k).wait_recv()
         grad = terms[core, q, chip].astype(f32) + from_mate[q, chip].astype(f32)
         for k in order:
             grad = grad + from_chip[q, k - 1].astype(f32)
         raised = momentum_decay * stack(mom[:, cols(q)]) + grad
-        picked = split_dot(raised, table[0]) * mask[q * tiles * rows:(q + 1) * tiles * rows, :]
+        picked = split_dot(raised, table[0]) * mask[pl.ds(pl.multiple_of(q * tiles * rows, tiles * rows), tiles * rows), :]
         sent[q] = picked.astype(bf16)
         for k in range(1, n_site):
             site_copy(q, k).start()
         kept = raised - split_dot(picked, table[1])
-        mom_new[:, cols(q)] = unstack(kept, rows)
-        mom_store(q).start()
-
-    def mom_store(q):
-        return pltpu.make_async_copy(
-            mom_new.at[:, cols(q)], mom_out_hbm.at[0, :, cols(q)], out_sem.at[q]
-        )
+        mom_out[0, :, cols(q)] = unstack(kept, rows)
 
     def update(q):
         for k in range(1, n_site):
             site_copy(q, k).wait_recv()
-        if q == 0:
-            weight_load.wait()
         total = sent[q].astype(f32)
         for k in range(1, n_site):
             total = total + from_site[q, k - 1].astype(f32)
@@ -240,7 +224,7 @@
             row_arrival(q, k).wait_recv()
             pass_copy(q, k).start()
 
-    def project(q, scores):
+    def project(q):
         row_arrival(q, 0).wait_recv()
         for k in range(1, chips):
             pass_arrival(q, k).wait_recv()
@@ -249,27 +233,35 @@
             [held[:, t * rows:(t + 1) * rows, :].reshape(n_dev * rows, LANES) for t in range(tiles)],
             axis=1,
         ).astype(bf16)
-        return scores + lax.dot_general(
+        total_scores[...] += lax.dot_general(
             held, tok[:, cols(q)], (((1,), (1,)), ((), ())), preferred_element_type=f32
         )
 
-    scores = jnp.zeros(score_out.shape[1:], f32)
-    for q in range(CHUNKS):
-        multiply(q)
-    for q in range(CHUNKS):
-        add_mate(q)
+    def each(count, body):
+        def step(at, carry):
+            body(at)
+            return carry
+        lax.fori_loop(0, count, step, 0)
+
+    def staggered(step):
+        for stage, shift in ((pick, 0), (update, 2), (hand_on, 4), (project, 5)):
+            @pl.when((step >= shift) & (step < shift + CHUNKS))
+            def _():
+                stage(step - shift)
+
+    total_scores[...] = jnp.zeros(total_scores.shape, f32)
+    cotan_load.wait()
+    pl.semaphore_wait(barrier, chips + n_site - 1)
+    each(CHUNKS, multiply)
+    each(CHUNKS, add_mate)
     make_mask()
-    for step in range(CHUNKS + 5):
-        if step < CHUNKS:
-            pick(step)
-        for stage, shift in ((update, 2), (hand_on, 4)):
-            if 0 <= step - shift < CHUNKS:
-                stage(step - shift)
-        if 0 <= step - 5 < CHUNKS:
-            scores = project(step - 5, scores)
-    score_out[0] = scores.astype(bf16)
-
-    for q in range(CHUNKS):
+    mom_load.wait()
+    table_load.wait()
+    weight_load.wait()
+    each(CHUNKS + 5, staggered)
+    score_out[0] = total_scores[...].astype(bf16)
+
+    def drain(q):
         mate_copy(q).wait_send()
         for k in range(1, chips):
             chip_copy(q, k).wait_send()
@@ -278,7 +270,8 @@
         row_copy(q, 0).wait_send()
         for k in range(1, n_site):
             site_copy(q, k).wait_send()
-        mom_store(q).wait()
+
+    each(CHUNKS, drain)
 
 
 def shards(n_dev, n_site, tokens, cotangent, weight, momentum, kept_index):
@@ -295,11 +288,11 @@
     scores, momentum_new = pl.pallas_call(
         functools.partial(kernel, n_dev, n_site),
         out_shape=(
-            jax.ShapeDtypeStruct((1, out_rows, count), bf16),
-            jax.ShapeDtypeStruct(momentum.shape, f32),
+            pltpu.VMEM((1, out_rows, count), bf16),
+            pltpu.VMEM(momentum.shape, f32),
         ),
         in_specs=[hbm] * 6,
-        out_specs=(vmem, hbm),
+        out_specs=(vmem, vmem),
         scratch_shapes=[
             pltpu.VMEM((out_rows, count), bf16),
             pltpu.VMEM((rows, width), bf16),
@@ -308,7 +301,7 @@
             pltpu.VMEM((rows, width), f32),
             pltpu.VMEM((rows, kept, width // SPAN), jnp.int32),
             pltpu.VMEM((high * CHUNKS, LANES), f32),
-            pltpu.VMEM((rows, width), f32),
+            pltpu.VMEM((out_rows, count), f32),
             pltpu.VMEM((2, CHUNKS, chips, high, LANES), bf16),
             pltpu.VMEM((CHUNKS, chips, high, LANES), bf16),
             pltpu.VMEM((CHUNKS, chips, high, LANES), bf16),
@@ -316,7 +309,7 @@
             pltpu.VMEM((CHUNKS, high, LANES), bf16),
             pltpu.VMEM((CHUNKS, n_site - 1, high, LANES), bf16),
             pltpu.VMEM((CHUNKS, n_dev, high, LANES), bf16),
-            sems, sems, sems, sems((CHUNKS,)), sems, sems, sems((CHUNKS,)),
+            sems, sems, sems, sems((CHUNKS,)), sems, sems,
             sems((CHUNKS,)), sems((CHUNKS,)),
             sems((CHUNKS, chips - 1)), sems((CHUNKS, chips - 1)),
             sems((CHUNKS, n_site - 1)), sems((CHUNKS, n_site - 1)),

time: 33.7 us -> 31.4 us (0.932)
  local copies, waits for them, and re-layouts: 2.99 us -> 1.31 us
  Pallas kernels: 29.8 us -> 29.3 us
    unnamed x2, local copies, waits for them, and re-layouts: 2.99 us -> 1.31 us
    pallas_call x1, Pallas kernels: 29.8 us -> 29.3 us  [shards(): pl.pallas_call(functools.partial(kernel, n_dev, n_site), out_shape=(pltpu...]
where the time goes in v4:
time: 31.4 us; the launch traced here: 31.3 us
  Pallas kernels  29.3 us (93%)
  local copies, waits for them, and re-layouts  1.31 us (4%)
  between operations  0.64 us (2%)
    pallas_call x1, Pallas kernels, shards(): pl.pallas_call(functools.partial(kernel, n_dev, n_site), out_shape=(pltpu...  29.3 us
    unnamed x2, local copies, waits for them, and re-layouts  1.31 us

profile of v4, /device:TPU:1, one launch (start us, length us, event | category | flops | bytes accessed | tf_op | source)
XLA Modules:
  0.0 31.3 jit_solution(7583502254020993212)
XLA Ops:
  0.6 29.3 %shard_map.77 = (bf16[1,64,128]{2,1,0:T(8,128)(2,1)S(1)}, f32[1,8,8192]{2,1,0:T(8,128)S(1)}) custom-call(bf16[1,128,8192]{2,1,0:T(8,128)(2,1)} %tok_hbm.1, bf16[64,128]{1,0:T(8,128)(2,1)} %bitcast.7, bf16[8,8192]{1,0:T(8,128)(2,1)} %weight_hbm.1, f32[1,8,8192]{2,1,0:T(8,128)} %mom_hbm.1, s32[4,8,16,128]{3,2,1,0:T(8,128)} %bitcast.6, ...), custom_call_target="tpu_custom_call" | custom-call | flops 268435456 | bytes 4194304 | tf_op jit(solution)/shard_map/pallas_call | solution.py:288
  30.0 0.6 %copy.10 = bf16[1,128,64]{1,2,0:T(8,128)(2,1)} copy(bf16[1,128,64]{1,2,0:T(8,128)(2,1)S(1)} %bitcast.5) | data formatting | bytes 32768
  30.6 0.7 %copy.11 = f32[1,8,8192]{2,1,0:T(8,128)} copy(f32[1,8,8192]{2,1,0:T(8,128)S(1)} %get-tuple-element.7) | data formatting | bytes 524288

commit v5 on v4

--- a/solution.py
+++ b/solution.py
@@ -98,14 +98,14 @@
     def tok_load(q):
         return pltpu.make_async_copy(tok_hbm.at[0, :, cols(q)], tok.at[:, cols(q)], tok_sem.at[q])
 
+    index_load = pltpu.make_async_copy(index_hbm.at[site], index, index_sem)
+    index_load.start()
     cotan_load = pltpu.make_async_copy(cotan_hbm, cotan, cotan_sem)
     weight_load = pltpu.make_async_copy(weight_hbm, weight, weight_sem)
     table_load = pltpu.make_async_copy(table_hbm, table, table_sem)
     cotan_load.start()
     for q in range(CHUNKS):
         tok_load(q).start()
-    index_load = pltpu.make_async_copy(index_hbm.at[site], index, index_sem)
-    index_load.start()
     mom_load = pltpu.make_async_copy(mom_hbm.at[0], mom, mom_sem)
     mom_load.start()
     table_load.start()
@@ -162,6 +162,10 @@
                 [part[:, :, t * LANES:(t + 1) * LANES] for t in range(tiles)], axis=1
             )
             terms[c, q] = part.astype(bf16)
+
+        @pl.when(q == 0)
+        def _():
+            pl.semaphore_wait(barrier, chips + n_site - 1)
         mate_copy(q).start()
 
     def add_mate(q):
@@ -250,11 +254,10 @@
                 stage(step - shift)
 
     total_scores[...] = jnp.zeros(total_scores.shape, f32)
+    make_mask()
     cotan_load.wait()
-    pl.semaphore_wait(barrier, chips + n_site - 1)
     each(CHUNKS, multiply)
     each(CHUNKS, add_mate)
-    make_mask()
     mom_load.wait()
     table_load.wait()
     weight_load.wait()

time: 31.4 us -> 33.6 us (1.070)
  Pallas kernels: 29.3 us -> 31.5 us
    pallas_call x1, Pallas kernels: 29.3 us -> 31.5 us  [shards(): pl.pallas_call(functools.partial(kernel, n_dev, n_site), out_shape=(pltpu...]
where the time goes in v5:
time: 33.6 us; the launch traced here: 33.4 us
  Pallas kernels  31.5 us (94%)
  local copies, waits for them, and re-layouts  1.31 us (4%)
  between operations  0.64 us (2%)
    pallas_call x1, Pallas kernels, shards(): pl.pallas_call(functools.partial(kernel, n_dev, n_site), out_shape=(pltpu...  31.5 us
    unnamed x2, local copies, waits for them, and re-layouts  1.31 us

profile of v5, /device:TPU:1, one launch (start us, length us, event | category | flops | bytes accessed | tf_op | source)
XLA Modules:
  0.0 33.4 jit_solution(12845621107986919276)
XLA Ops:
  0.6 31.5 %shard_map.77 = (bf16[1,64,128]{2,1,0:T(8,128)(2,1)S(1)}, f32[1,8,8192]{2,1,0:T(8,128)S(1)}) custom-call(bf16[1,128,8192]{2,1,0:T(8,128)(2,1)} %tok_hbm.1, bf16[64,128]{1,0:T(8,128)(2,1)} %bitcast.7, bf16[8,8192]{1,0:T(8,128)(2,1)} %weight_hbm.1, f32[1,8,8192]{2,1,0:T(8,128)} %mom_hbm.1, s32[4,8,16,128]{3,2,1,0:T(8,128)} %bitcast.6, ...), custom_call_target="tpu_custom_call" | custom-call | flops 268435456 | bytes 4194304 | tf_op jit(solution)/shard_map/pallas_call | solution.py:291
  32.1 0.6 %copy.10 = bf16[1,128,64]{1,2,0:T(8,128)(2,1)} copy(bf16[1,128,64]{1,2,0:T(8,128)(2,1)S(1)} %bitcast.5) | data formatting | bytes 32768
  32.7 0.7 %copy.11 = f32[1,8,8192]{2,1,0:T(8,128)} copy(f32[1,8,8192]{2,1,0:T(8,128)S(1)} %get-tuple-element.7) | data formatting | bytes 524288

commit v6 on v4

--- a/solution.py
+++ b/solution.py
@@ -171,17 +171,20 @@
         for k in order:
             chip_copy(q, k).start()
 
-    def make_mask():
+    def mask_words():
         index_load.wait()
         held = index[...]
         one = jnp.int32(1)
         low = jnp.sum(jnp.where(held < 32, one << (held & 31), 0), axis=1)
         high = jnp.sum(jnp.where(held >= 32, one << (held & 31), 0), axis=1)
+        return low, high
+
+    def make_mask(q, low, high):
         lane = lax.broadcasted_iota(jnp.int32, (rows, LANES), 1)
         first = lane < SPAN
         lower = (lane % SPAN) < 32
         shift = lane % 32
-        for t in range(width // LANES):
+        for t in range(q * tiles, (q + 1) * tiles):
             def word(block):
                 return jnp.where(
                     lower,
@@ -244,6 +247,10 @@
         lax.fori_loop(0, count, step, 0)
 
     def staggered(step):
+        for q in range(1, CHUNKS):
+            @pl.when(step == q)
+            def _():
+                make_mask(q, low, high)
         for stage, shift in ((pick, 0), (update, 2), (hand_on, 4), (project, 5)):
             @pl.when((step >= shift) & (step < shift + CHUNKS))
             def _():
@@ -254,7 +261,8 @@
     pl.semaphore_wait(barrier, chips + n_site - 1)
     each(CHUNKS, multiply)
     each(CHUNKS, add_mate)
-    make_mask()
+    low, high = mask_words()
+    make_mask(0, low, high)
     mom_load.wait()
     table_load.wait()
     weight_load.wait()

time: 31.4 us -> 31.4 us (level)
  no operation moved by 1% of the time
where the time goes in v6:
time: 31.4 us; the launch traced here: 31.3 us
  Pallas kernels  29.3 us (93%)
  local copies, waits for them, and re-layouts  1.31 us (4%)
  between operations  0.64 us (2%)
    pallas_call x1, Pallas kernels, shards(): pl.pallas_call(functools.partial(kernel, n_dev, n_site), out_shape=(pltpu...  29.3 us
    unnamed x2, local copies, waits for them, and re-layouts  1.31 us

profile of v6, /device:TPU:1, one launch (start us, length us, event | category | flops | bytes accessed | tf_op | source)
XLA Modules:
  0.0 31.3 jit_solution(8572330090304681465)
XLA Ops:
  0.6 29.3 %shard_map.77 = (bf16[1,64,128]{2,1,0:T(8,128)(2,1)S(1)}, f32[1,8,8192]{2,1,0:T(8,128)S(1)}) custom-call(bf16[1,128,8192]{2,1,0:T(8,128)(2,1)} %tok_hbm.1, bf16[64,128]{1,0:T(8,128)(2,1)} %bitcast.7, bf16[8,8192]{1,0:T(8,128)(2,1)} %weight_hbm.1, f32[1,8,8192]{2,1,0:T(8,128)} %mom_hbm.1, s32[4,8,16,128]{3,2,1,0:T(8,128)} %bitcast.6, ...), custom_call_target="tpu_custom_call" | custom-call | flops 268435456 | bytes 4194304 | tf_op jit(solution)/shard_map/pallas_call | solution.py:296
  30.0 0.6 %copy.10 = bf16[1,128,64]{1,2,0:T(8,128)(2,1)} copy(bf16[1,128,64]{1,2,0:T(8,128)(2,1)S(1)} %bitcast.5) | data formatting | bytes 32768
  30.6 0.7 %copy.11 = f32[1,8,8192]{2,1,0:T(8,128)} copy(f32[1,8,8192]{2,1,0:T(8,128)S(1)} %get-tuple-element.7) | data formatting | bytes 524288
